TPU v7x, 256 devices: a whole 4x4x8 slice. The times are simulated.
256 devices in a mesh: dp: 8 (over x, z_lo), pipe: 4 (over y), tensor: 8 (over z_hi, core).
Axes of the slice: x: 4, y: 4, z: 8 (z_hi: 4, z_lo: 2; z = z_hi * 2 + z_lo), core: 2. Of those that a mesh axis runs over, the one named last changes fastest.
Arguments:
- h_in: bfloat16 [2, 96, 8192], P(None, 'dp', 'tensor'), may hold values from -6 to 6
- cotangent: bfloat16 [2, 96, 8192], P(None, 'dp', 'tensor'), may hold values from -1 to 1
- w_up: bfloat16 [4, 8192, 14336], P('pipe', 'tensor', 'dp'), may hold values from -0.0625 to 0.0625
- w_down: bfloat16 [4, 14336, 8192], P('pipe', 'dp', 'tensor'), may hold values from -0.046875 to 0.046875
- a_up: bfloat16 [4, 8192, 256], P('pipe', 'tensor'), may hold values from -0.0625 to 0.0625
- b_up: bfloat16 [4, 256, 14336], P('pipe', None, 'dp'), may hold values from -0.75 to 0.75
- a_down: bfloat16 [4, 14336, 256], P('pipe', 'dp'), may hold values from -0.046875 to 0.046875
- b_down: bfloat16 [4, 256, 8192], P('pipe', None, 'tensor'), may hold values from -0.75 to 0.75
- job_ids: int32 [2, 8], replicated, may hold values from 0 to 3
- ranks: int32 [4], replicated, may hold values from 8 to 64
Outputs:
- grad_a_up: float32 [4, 8192, 256], P('pipe', 'tensor')
- grad_b_up: float32 [4, 256, 14336], P('pipe', 'tensor', 'dp')
- grad_a_down: float32 [4, 14336, 256], P('pipe', 'dp', 'tensor')
- grad_b_down: float32 [4, 256, 8192], P('pipe', None, 'tensor')
All inputs are finite; a program needn't handle non-finite values.
Results may differ from a plain program's by a relative error of at most 0.025.
Values may be sent and summed in bfloat16 or wider, within the bound.
No kernel may reach another device: no remote copies, remote signals or barrier semaphores. Data moves between devices by JAX's collectives and lax.ppermute only.
A program may use at most 128 MiB of HBM per device.

v0:
```python
import jax
import jax.numpy as jnp
from jax import lax
from jax.sharding import PartitionSpec as P

D = 8192
RMAX = 64
JOBS = 4
MB = 2
SEQ_LEN = 12


EPS = 1e-05
ALPHA = 16.0


def from_behind(block, axis, distance):
    devices = range(lax.axis_size(axis))
    route = [(i - distance, i) for i in devices if i - distance in devices]
    return lax.ppermute(block, axis, route)


def column_weights(ranks, lanes):
    column = jnp.arange(lanes, dtype=jnp.int32)
    col_job = column // RMAX
    picked = col_job[:, None] == jnp.arange(JOBS, dtype=jnp.int32)[None, :]
    rank_col = jnp.sum(jnp.where(picked, ranks[None, :], 0), axis=1)
    scale = jnp.where(
        column % RMAX < rank_col, ALPHA / rank_col.astype(jnp.float32), jnp.float32(0.0)
    )
    return (col_job, scale)


def row_mask(seq_jobs, col_job, scale):
    job_row = jnp.broadcast_to(seq_jobs[:, None], (seq_jobs.shape[0], SEQ_LEN)).reshape(-1)
    return jnp.where(job_row[:, None] == col_job[None, :], scale[None, :], jnp.float32(0.0))


def silu_grad(u):
    sig = jax.nn.sigmoid(u)
    return sig * (1.0 + u * (1.0 - sig))


def mm(left, right):
    return jnp.dot(left, right, preferred_element_type=jnp.float32)


def mm_last(left, right):
    return lax.dot_general(
        left, right, (((1,), (1,)), ((), ())), preferred_element_type=jnp.float32
    )


def mm_first(left, right):
    return lax.dot_general(
        left, right, (((0,), (0,)), ((), ())), preferred_element_type=jnp.float32
    )


def gather_rows(value):
    return lax.all_gather(value, "dp", axis=0, tiled=True)


def row_sums(first, second):
    return (
        lax.psum_scatter(first, "dp", scatter_dimension=0, tiled=True),
        lax.psum_scatter(second, "dp", scatter_dimension=0, tiled=True),
    )


def handoff(value, step):
    return from_behind(value, "pipe", step)


def per_device(h_in, cotangent, w_up, w_down, a_up, b_up, a_down, b_down, job_ids, ranks):
    wu, wd, au, bu, ad, bd = (w_up[0], w_down[0], a_up[0], b_up[0], a_down[0], b_down[0])
    rows = h_in.shape[1]
    width = h_in.shape[2]
    hidden = wu.shape[1]
    lanes = au.shape[1]
    replicas = lax.axis_size("dp")
    sections = lax.axis_size("pipe")
    section = lax.axis_index("pipe")
    tokens = rows * replicas
    start = lax.axis_index("dp") * rows
    col_job, scale = column_weights(ranks, lanes)
    ticks = MB + sections - 1

    def masks(m_c):
        mask = row_mask(lax.dynamic_index_in_dim(job_ids, m_c, 0, keepdims=False), col_job, scale)
        return (mask, lax.dynamic_slice_in_dim(mask, start, rows, 0))

    buffers = (
        jnp.zeros((MB, tokens, width), jnp.bfloat16),
        jnp.zeros((MB, tokens), jnp.float32),
        jnp.zeros((MB, tokens, hidden), jnp.float32),
        jnp.zeros((MB, tokens, hidden), jnp.bfloat16),
        jnp.zeros((MB, tokens, lanes), jnp.bfloat16),
        jnp.zeros((MB, rows, lanes), jnp.bfloat16),
    )
    received = jnp.zeros((rows, width), jnp.bfloat16)
    for tick in range(ticks):
        batch = tick - section
        valid = (batch >= 0) & (batch < MB)
        m_c = jnp.clip(batch, 0, MB - 1)
        x_in = jnp.where(
            section == 0, lax.dynamic_index_in_dim(h_in, m_c, 0, keepdims=False), received
        )
        forward_mask, forward_mask_own = masks(m_c)
        forward_gathered = gather_rows(x_in)
        partial_up = mm(forward_gathered, wu)
        partial_q = mm(forward_gathered, au)
        partial_ss = jnp.sum(jnp.square(forward_gathered.astype(jnp.float32)), axis=1)
        share = tokens // lax.axis_size("tensor")
        share_up = lax.psum_scatter(partial_up, "tensor", scatter_dimension=0, tiled=True)
        share_q = lax.psum_scatter(partial_q, "tensor", scatter_dimension=0, tiled=True)
        share_ss = lax.psum_scatter(partial_ss, "tensor", scatter_dimension=0, tiled=True)
        mask_share = lax.dynamic_slice_in_dim(
            forward_mask, lax.axis_index("tensor") * share, share, 0
        )
        rs_share = lax.rsqrt(share_ss / D + EPS)
        masked_q = share_q * mask_share
        summed_share = share_up + mm(masked_q.astype(jnp.bfloat16), bu)
        forward_summed = lax.all_gather(summed_share, "tensor", axis=0, tiled=True)
        masked_all = lax.all_gather(masked_q, "tensor", axis=0, tiled=True)
        forward_rs = lax.all_gather(rs_share, "tensor", axis=0, tiled=True)
        forward_qb = masked_all.astype(jnp.bfloat16)
        forward_u = forward_rs[:, None] * forward_summed
        forward_act = jax.nn.silu(forward_u).astype(jnp.bfloat16)
        y_own, r_own = row_sums(mm(forward_act, wd), mm(forward_act, ad))
        forward_rb = (r_own * forward_mask_own).astype(jnp.bfloat16)
        h_next = (x_in.astype(jnp.float32) + y_own + mm(forward_rb, bd)).astype(jnp.bfloat16)
        h_next, fresh = (
            h_next,
            (forward_gathered, forward_rs, forward_summed, forward_act, forward_qb, forward_rb),
        )
        buffers = tuple(
            (
                lax.dynamic_update_index_in_dim(
                    old,
                    jnp.where(valid, new, lax.dynamic_index_in_dim(old, m_c, 0, keepdims=False)),
                    m_c,
                    0,
                )
                for old, new in zip(buffers, fresh)
            )
        )
        received = handoff(jnp.where(valid, h_next, jnp.zeros_like(h_next)), 1)
    grads = (
        jnp.zeros((width, lanes), jnp.float32),
        jnp.zeros((lanes, width), jnp.float32),
        jnp.zeros((lanes, hidden), jnp.float32),
        jnp.zeros((hidden, lanes), jnp.float32),
    )
    received = jnp.zeros((rows, width), jnp.bfloat16)
    for tick in range(ticks):
        batch = tick - (sections - 1 - section)
        valid = (batch >= 0) & (batch < MB)
        weight_on = valid.astype(jnp.float32)
        m_c = jnp.clip(batch, 0, MB - 1)
        g_in = jnp.where(
            section == sections - 1,
            lax.dynamic_index_in_dim(cotangent, m_c, 0, keepdims=False),
            received,
        )
        backward_grads = grads
        backward_grad_au, backward_grad_bd, backward_grad_bu, backward_grad_ad = backward_grads
        backward_mask, mask_own = masks(m_c)
        gathered, rs, summed, act, qb, rb = tuple(
            (lax.dynamic_index_in_dim(buf, m_c, 0, keepdims=False) for buf in buffers)
        )
        grad_rows = gather_rows(g_in)
        d_act_sum, d_r = lax.psum((mm_last(grad_rows, wd), mm_last(grad_rows, bd)), "tensor")
        d_rb = (d_r * backward_mask).astype(jnp.bfloat16)
        d_act = d_act_sum + mm_last(d_rb, ad)
        u = rs[:, None] * summed
        d_u = d_act * silu_grad(u)
        d_sb = (d_u * rs[:, None]).astype(jnp.bfloat16)
        rowdot = jnp.sum(d_u * summed, axis=1)
        part_x = (
            mm_last(d_sb, wu)
            - gathered.astype(jnp.float32) * (rs**3 / D)[:, None] * rowdot[:, None]
        )
        d_x_own, d_q_own = row_sums(part_x, mm_last(d_sb, bu))
        d_qb = (d_q_own * mask_own).astype(jnp.bfloat16)
        x_own = lax.dynamic_slice_in_dim(gathered, start, rows, 0)
        d_x = g_in.astype(jnp.float32) + d_x_own + mm_last(d_qb, au)
        backward_grads = (
            backward_grad_au + weight_on * mm_first(x_own, d_qb),
            backward_grad_bd + weight_on * mm_first(rb, g_in),
            backward_grad_bu + weight_on * mm_first(qb, d_sb),
            backward_grad_ad + weight_on * mm_first(act, d_rb),
        )
        d_x, grads = (d_x.astype(jnp.bfloat16), backward_grads)
        received = handoff(jnp.where(valid, d_x, jnp.zeros_like(d_x)), -1)
    grad_au, grad_bd, grad_bu, grad_ad = grads
    grad_au, grad_bd = lax.psum((grad_au, grad_bd), "dp")
    piece = lanes // lax.axis_size("tensor")
    offset = lax.axis_index("tensor") * piece
    grad_bu_own = lax.dynamic_slice_in_dim(grad_bu, offset, piece, 0)
    grad_ad_own = lax.dynamic_slice_in_dim(grad_ad, offset, piece, 1)
    return (grad_au[None], grad_bu_own[None], grad_ad_own[None], grad_bd[None])


def solution(mesh):
    in_specs = (
        P(None, "dp", "tensor"),
        P(None, "dp", "tensor"),
        P("pipe", "tensor", "dp"),
        P("pipe", "dp", "tensor"),
        P("pipe", "tensor", None),
        P("pipe", None, "dp"),
        P("pipe", "dp", None),
        P("pipe", None, "tensor"),
        P(),
        P(),
    )
    out_specs = (
        P("pipe", "tensor", None),
        P("pipe", "tensor", "dp"),
        P("pipe", "dp", "tensor"),
        P("pipe", None, "tensor"),
    )
    return jax.shard_map(
        per_device, mesh=mesh, in_specs=in_specs, out_specs=out_specs, check_vma=False
    )
```

profile of v0, /device:TPU:1, one launch (start us, length us, event | category | flops | bytes accessed | tf_op | source)
XLA Modules:
  0.0 1875.6 jit_solution(6378137066493261440)
XLA Ops:
  9.3 25.0 %all-gather = bf16[1,96,1024]{2,0,1:T(2,128)(2,1)S(1)} all-gather(bf16[1,12,1024]{2,0,1:T(2,128)(2,1)S(1)} %copy.51), channel_id=2, replica_groups=mesh['dp'=8,'pipe'=4,'tensor'=8] {'dp'}, dimensions={1}, use_global_device_ids=true | all-gather | bytes 221184 | tf_op jit(solution)/shard_map/all_gather | solution.py:61
  38.5 25.7 %fusion.411 = (f32[16,1792]{1,0:T(8,128)S(1)}, f32[16,256]{1,0:T(8,128)S(1)}) fusion(f32[96,1792]{1,0:T(8,128)S(1)} %fusion.62, f32[96,256]{1,0:T(8,128)S(1)} %fusion.166), kind=kCustom, calls=%all-reduce-scatter.32 | all-reduce-scatter fusion | flops 262145 | bytes 918528
  81.9 23.9 %all-gather.1 = bf16[1,96,1024]{2,0,1:T(2,128)(2,1)S(1)} all-gather(bf16[1,12,1024]{2,0,1:T(2,128)(2,1)S(1)} %copy.57), channel_id=3, replica_groups=mesh['dp'=8,'pipe'=4,'tensor'=8] {'dp'}, dimensions={1}, use_global_device_ids=true | all-gather | bytes 221184 | tf_op jit(solution)/shard_map/all_gather | solution.py:61
  249.6 24.3 %all-gather.3 = bf16[8,12,1024]{2,1,0:T(8,128)(2,1)} all-gather(bf16[1,12,1024]{2,1,0:T(8,128)(2,1)S(1)} %fusion.402), channel_id=1, replica_groups=mesh['dp'=8,'pipe'=4,'tensor'=8] {'dp'}, dimensions={0}, use_global_device_ids=true | all-gather | bytes 221184 | tf_op jit(solution)/shard_map/all_gather | solution.py:61
  280.0 32.4 %fusion.410 = (f32[16,1792]{1,0:T(8,128)}, f32[16,256]{1,0:T(8,128)S(1)}) fusion(f32[96,1792]{1,0:T(8,128)} %fusion.60, f32[96,256]{1,0:T(8,128)} %fusion.164), kind=kCustom, calls=%all-reduce-scatter.31 | all-reduce-scatter fusion | flops 262145 | bytes 918528
  416.7 23.1 %fusion.419 = (f32[16,256]{1,0:T(8,128)S(1)}, f32[16,1024]{1,0:T(8,128)S(1)}) fusion(f32[96,256]{1,0:T(8,128)} %fusion.104, f32[96,1024]{1,0:T(8,128)} %fusion.42), kind=kCustom, calls=%all-reduce-scatter.40 | all-reduce-scatter fusion | flops 163841 | bytes 574464
  471.7 24.3 %all-gather.5 = bf16[8,12,1024]{2,1,0:T(8,128)(2,1)} all-gather(bf16[1,12,1024]{2,1,0:T(8,128)(2,1)S(1)} %fusion.403), channel_id=1, replica_groups=mesh['dp'=8,'pipe'=4,'tensor'=8] {'dp'}, dimensions={0}, use_global_device_ids=true | all-gather | bytes 221184 | tf_op jit(solution)/shard_map/all_gather | solution.py:61
  502.2 31.6 %fusion.409 = (f32[16,1792]{1,0:T(8,128)}, f32[16,256]{1,0:T(8,128)S(1)}) fusion(f32[96,1792]{1,0:T(8,128)} %fusion.58, f32[96,256]{1,0:T(8,128)} %fusion.162), kind=kCustom, calls=%all-reduce-scatter.30 | all-reduce-scatter fusion | flops 262145 | bytes 918528
  690.1 24.3 %all-gather.7 = bf16[8,12,1024]{2,1,0:T(8,128)(2,1)} all-gather(bf16[1,12,1024]{2,1,0:T(8,128)(2,1)S(1)} %fusion.404), channel_id=1, replica_groups=mesh['dp'=8,'pipe'=4,'tensor'=8] {'dp'}, dimensions={0}, use_global_device_ids=true | all-gather | bytes 221184 | tf_op jit(solution)/shard_map/all_gather | solution.py:61
  720.6 32.1 %fusion.408 = (f32[16,1792]{1,0:T(8,128)}, f32[16,256]{1,0:T(8,128)S(1)}) fusion(f32[96,1792]{1,0:T(8,128)} %fusion.56, f32[96,256]{1,0:T(8,128)} %fusion.160), kind=kCustom, calls=%all-reduce-scatter.29 | all-reduce-scatter fusion | flops 262145 | bytes 918528
  890.5 25.1 %all-gather.9 = bf16[8,12,1024]{2,1,0:T(8,128)(2,1)} all-gather(bf16[1,12,1024]{2,1,0:T(8,128)(2,1)S(1)} %fusion.254), channel_id=1, replica_groups=mesh['dp'=8,'pipe'=4,'tensor'=8] {'dp'}, dimensions={0}, use_global_device_ids=true | all-gather | bytes 221184 | tf_op jit(solution)/shard_map/all_gather | solution.py:61
  921.2 24.1 %all-reduce.25 = f32[96]{0:T(128)S(1)} all-reduce(f32[96]{0:T(128)S(1)} %multiply_reduce_fusion), channel_id=24, replica_groups=mesh['dp'=8,'pipe'=4,'tensor'=8] {'tensor'}, use_global_device_ids=true, to_apply=%region_28.29.clone | all-reduce | flops 96 | bytes 768
  1032.4 22.0 %fusion.416 = (f32[16,256]{1,0:T(8,128)S(1)}, f32[16,1024]{1,0:T(8,128)S(1)}) fusion(f32[96,256]{1,0:T(8,128)} %fusion.116, f32[96,1024]{1,0:T(8,128)} %fusion.81), kind=kCustom, calls=%all-reduce-scatter.37 | all-reduce-scatter fusion | flops 163841 | bytes 574464
  1084.1 24.8 %all-gather.11 = bf16[8,12,1024]{2,1,0:T(8,128)(2,1)} all-gather(bf16[1,12,1024]{2,1,0:T(8,128)(2,1)S(1)} %bitcast.705), channel_id=1, replica_groups=mesh['dp'=8,'pipe'=4,'tensor'=8] {'dp'}, dimensions={0}, use_global_device_ids=true | all-gather | bytes 221184 | tf_op jit(solution)/shard_map/all_gather | solution.py:61
  1121.5 28.0 %all-gather.18 = bf16[8,12,256]{2,1,0:T(8,128)(2,1)S(1)} all-gather(bf16[1,12,256]{2,1,0:T(8,128)(2,1)S(1)} %fusion.359), channel_id=1, replica_groups=mesh['dp'=8,'pipe'=4,'tensor'=8] {'tensor'}, dimensions={0}, use_global_device_ids=true | all-gather | bytes 55296 | tf_op jit(solution)/shard_map/all_gather | solution.py:125
  1149.5 48.7 %all-reduce.99.cloned.1.call-done = (f32[96,1792]{1,0:T(8,128)}, f32[96,256]{1,0:T(8,128)}) async-done(((f32[96,1792]{1,0:T(8,128)}, f32[96,256]{1,0:T(8,128)}), (f32[96,1792]{1,0:T(8,128)}, f32[96,256]{1,0:T(8,128)})) %all-reduce.99.cloned.1.call-update) | async-done | bytes 786448 | tf_op jit(solution)/shard_map/psum | solution.py:173
  1251.5 25.0 %all-gather.12 = bf16[8,12,1024]{2,1,0:T(8,128)(2,1)} all-gather(bf16[1,12,1024]{2,1,0:T(8,128)(2,1)S(1)} %bitcast.706), channel_id=1, replica_groups=mesh['dp'=8,'pipe'=4,'tensor'=8] {'dp'}, dimensions={0}, use_global_device_ids=true | all-gather | bytes 221184 | tf_op jit(solution)/shard_map/all_gather | solution.py:61
  1290.3 29.3 %all-gather.19 = bf16[8,12,256]{2,1,0:T(8,128)(2,1)S(1)} all-gather(bf16[1,12,256]{2,1,0:T(8,128)(2,1)S(1)} %fusion.357), channel_id=1, replica_groups=mesh['dp'=8,'pipe'=4,'tensor'=8] {'tensor'}, dimensions={0}, use_global_device_ids=true | all-gather | bytes 55296 | tf_op jit(solution)/shard_map/all_gather | solution.py:125
  1320.3 48.8 %all-reduce.97.cloned.1.call-done = (f32[96,1792]{1,0:T(8,128)}, f32[96,256]{1,0:T(8,128)}) async-done(((f32[96,1792]{1,0:T(8,128)}, f32[96,256]{1,0:T(8,128)}), (f32[96,1792]{1,0:T(8,128)}, f32[96,256]{1,0:T(8,128)})) %all-reduce.97.cloned.1.call-update) | async-done | bytes 786448 | tf_op jit(solution)/shard_map/psum | solution.py:173
  1424.1 24.9 %all-gather.13 = bf16[8,12,1024]{2,1,0:T(8,128)(2,1)} all-gather(bf16[1,12,1024]{2,1,0:T(8,128)(2,1)S(1)} %bitcast.707), channel_id=1, replica_groups=mesh['dp'=8,'pipe'=4,'tensor'=8] {'dp'}, dimensions={0}, use_global_device_ids=true | all-gather | bytes 221184 | tf_op jit(solution)/shard_map/all_gather | solution.py:61
  1463.6 78.0 %all-reduce.95.cloned.1.call-done = (f32[96,1792]{1,0:T(8,128)}, f32[96,256]{1,0:T(8,128)}) async-done(((f32[96,1792]{1,0:T(8,128)}, f32[96,256]{1,0:T(8,128)}), (f32[96,1792]{1,0:T(8,128)}, f32[96,256]{1,0:T(8,128)})) %all-reduce.95.cloned.1.call-update) | async-done | bytes 786448 | tf_op jit(solution)/shard_map/psum | solution.py:173
  1599.9 23.0 %all-gather.14 = bf16[8,12,1024]{2,1,0:T(8,128)(2,1)S(1)} all-gather(bf16[1,12,1024]{2,1,0:T(8,128)(2,1)S(1)} %fusion.406), channel_id=1, replica_groups=mesh['dp'=8,'pipe'=4,'tensor'=8] {'dp'}, dimensions={0}, use_global_device_ids=true | all-gather | bytes 221184 | tf_op jit(solution)/shard_map/all_gather | solution.py:61
  1633.9 78.7 %all-reduce.93.cloned.1.call-done = (f32[96,1792]{1,0:T(8,128)}, f32[96,256]{1,0:T(8,128)}) async-done(((f32[96,1792]{1,0:T(8,128)}, f32[96,256]{1,0:T(8,128)}), (f32[96,1792]{1,0:T(8,128)}, f32[96,256]{1,0:T(8,128)})) %all-reduce.93.cloned.1.call-update) | async-done | bytes 786448 | tf_op jit(solution)/shard_map/psum | solution.py:173
  1760.9 102.8 %all-reduce.103.cloned.1.call-done = (f32[1,1024,256]{2,1,0:T(8,128)}, f32[1,256,1024]{2,1,0:T(8,128)}) async-done(((f32[1,1024,256]{2,1,0:T(8,128)}, f32[1,256,1024]{2,1,0:T(8,128)}), (f32[1,1024,256]{2,1,0:T(8,128)}, f32[1,256,1024]{2,1,0:T(8,128)})) %all-reduce.103.cloned.1.call-update) | async-done | bytes 2097168 | tf_op jit(solution)/shard_map/psum | solution.py:197
  (662 shorter events, 1006.7 us)
Async XLA Ops:
  7.2 1019.9 %all-reduce.101.cloned.1.call-start = ((), (), s32[]{:S(2)}) async-start(), calls=%async_computation.4 | async-start | bytes 1572864 | tf_op jit(solution)/shard_map/psum | solution.py:173
  64.2 89.6 %collective-permute-start.10 = (f32[16,256]{1,0:T(8,128)S(1)}, f32[16,256]{1,0:T(8,128)S(1)}, u32[]{:S(2)}, u32[]{:S(2)}) collective-permute-start(f32[16,256]{1,0:T(8,128)S(1)} %get-tuple-element.35), channel_id=1, source_target_pairs={{0,1},{1,2},{2,3},{3,4},{4,5},{5,6},{6,7},{8,9},{9,10},{10,11},{11... | collective-permute-start | bytes 49160
  67.9 85.3 %collective-permute-start.11 = (f32[12,256]{1,0:T(8,128)S(1)}, f32[12,256]{1,0:T(8,128)S(1)}, u32[]{:S(2)}, u32[]{:S(2)}) collective-permute-start(f32[12,256]{1,0:T(8,128)S(1)} %slice.1), channel_id=1, source_target_pairs={{0,2},{1,3},{2,4},{3,5},{4,6},{5,7},{8,10},{9,11},{10,12},{11,13},... | collective-permute-start | bytes 36872
  75.8 94.0 %collective-permute-start.8 = (f32[16,1792]{1,0:T(8,128)S(1)}, f32[16,1792]{1,0:T(8,128)}, u32[]{:S(2)}, u32[]{:S(2)}) collective-permute-start(f32[16,1792]{1,0:T(8,128)S(1)} %get-tuple-element.34), channel_id=1, source_target_pairs={{0,1},{1,2},{2,3},{3,4},{4,5},{5,6},{6,7},{8,9},{9,10},{10,11},{11... | collective-permute-start | bytes 344072
  78.6 91.1 %collective-permute-start.9 = (f32[12,1792]{1,0:T(8,128)}, f32[12,1792]{1,0:T(8,128)}, u32[]{:S(2)}, u32[]{:S(2)}) collective-permute-start(f32[12,1792]{1,0:T(8,128)} %slice), channel_id=1, source_target_pairs={{0,2},{1,3},{2,4},{3,5},{4,6},{5,7},{8,10},{9,11},{10,12},{11,13},... | collective-permute-start | bytes 258056
  111.0 1087.3 %all-reduce.99.cloned.1.call-start = ((), (), s32[]{:S(2)}) async-start(), calls=%async_computation.3 | async-start | bytes 1572864 | tf_op jit(solution)/shard_map/psum | solution.py:173
  312.4 52.1 %collective-permute-start.18 = (f32[16,256]{1,0:T(8,128)S(1)}, f32[16,256]{1,0:T(8,128)}, u32[]{:S(2)}, u32[]{:S(2)}) collective-permute-start(f32[16,256]{1,0:T(8,128)S(1)} %get-tuple-element.31), channel_id=1, source_target_pairs={{0,1},{1,2},{2,3},{3,4},{4,5},{5,6},{6,7},{8,9},{9,10},{10,11},{11... | collective-permute-start | bytes 49160
  317.2 67.9 %collective-permute-start.16 = (f32[16,1792]{1,0:T(8,128)}, f32[16,1792]{1,0:T(8,128)}, u32[]{:S(2)}, u32[]{:S(2)}) collective-permute-start(f32[16,1792]{1,0:T(8,128)} %get-tuple-element.30), channel_id=1, source_target_pairs={{0,1},{1,2},{2,3},{3,4},{4,5},{5,6},{6,7},{8,9},{9,10},{10,11},{11... | collective-permute-start | bytes 344072
  358.1 27.0 %collective-permute-start.17 = (f32[12,1792]{1,0:T(8,128)}, f32[12,1792]{1,0:T(8,128)}, u32[]{:S(2)}, u32[]{:S(2)}) collective-permute-start(f32[12,1792]{1,0:T(8,128)} %slice.4), channel_id=1, source_target_pairs={{0,2},{1,3},{2,4},{3,5},{4,6},{5,7},{8,10},{9,11},{10,12},{11,13},... | collective-permute-start | bytes 258056
  439.8 17.9 collective-permute-start.22
  442.9 19.7 %collective-permute-start.20 = (f32[16,1024]{1,0:T(8,128)S(1)}, f32[16,1024]{1,0:T(8,128)}, u32[]{:S(2)}, u32[]{:S(2)}) collective-permute-start(f32[16,1024]{1,0:T(8,128)S(1)} %get-tuple-element.67), channel_id=1, source_target_pairs={{0,32},{32,64},{64,96},{96,128},{128,160},{160,192},{192,224},{1,3... | collective-permute-start | bytes 196616
  533.8 55.1 %collective-permute-start.26 = (f32[16,256]{1,0:T(8,128)S(1)}, f32[16,256]{1,0:T(8,128)}, u32[]{:S(2)}, u32[]{:S(2)}) collective-permute-start(f32[16,256]{1,0:T(8,128)S(1)} %get-tuple-element.27), channel_id=1, source_target_pairs={{0,1},{1,2},{2,3},{3,4},{4,5},{5,6},{6,7},{8,9},{9,10},{10,11},{11... | collective-permute-start | bytes 49160
  538.3 68.5 %collective-permute-start.24 = (f32[16,1792]{1,0:T(8,128)}, f32[16,1792]{1,0:T(8,128)}, u32[]{:S(2)}, u32[]{:S(2)}) collective-permute-start(f32[16,1792]{1,0:T(8,128)} %get-tuple-element.26), channel_id=1, source_target_pairs={{0,1},{1,2},{2,3},{3,4},{4,5},{5,6},{6,7},{8,9},{9,10},{10,11},{11... | collective-permute-start | bytes 344072
  582.5 24.3 %collective-permute-start.25 = (f32[12,1792]{1,0:T(8,128)}, f32[12,1792]{1,0:T(8,128)}, u32[]{:S(2)}, u32[]{:S(2)}) collective-permute-start(f32[12,1792]{1,0:T(8,128)} %slice.8), channel_id=1, source_target_pairs={{0,2},{1,3},{2,4},{3,5},{4,6},{5,7},{8,10},{9,11},{10,12},{11,13},... | collective-permute-start | bytes 258056
  661.2 15.9 collective-permute-start.28
  752.7 54.3 %collective-permute-start.34 = (f32[16,256]{1,0:T(8,128)S(1)}, f32[16,256]{1,0:T(8,128)}, u32[]{:S(2)}, u32[]{:S(2)}) collective-permute-start(f32[16,256]{1,0:T(8,128)S(1)} %get-tuple-element.23), channel_id=1, source_target_pairs={{0,1},{1,2},{2,3},{3,4},{4,5},{5,6},{6,7},{8,9},{9,10},{10,11},{11... | collective-permute-start | bytes 49160
  756.2 52.3 %collective-permute-start.32 = (f32[16,1792]{1,0:T(8,128)}, f32[16,1792]{1,0:T(8,128)}, u32[]{:S(2)}, u32[]{:S(2)}) collective-permute-start(f32[16,1792]{1,0:T(8,128)} %get-tuple-element.22), channel_id=1, source_target_pairs={{0,1},{1,2},{2,3},{3,4},{4,5},{5,6},{6,7},{8,9},{9,10},{10,11},{11... | collective-permute-start | bytes 344072
  791.5 15.4 collective-permute-start.35
  863.1 16.3 collective-permute-start.36
  981.4 16.9 collective-permute-start.40
  1116.7 252.4 %all-reduce.97.cloned.1.call-start = ((), (), s32[]{:S(2)}) async-start(), calls=%async_computation.2 | async-start | bytes 1572864 | tf_op jit(solution)/shard_map/psum | solution.py:173
  1284.3 257.3 %all-reduce.95.cloned.1.call-start = ((), (), s32[]{:S(2)}) async-start(), calls=%async_computation.1 | async-start | bytes 1572864 | tf_op jit(solution)/shard_map/psum | solution.py:173
  1456.9 255.7 %all-reduce.93.cloned.1.call-start = ((), (), s32[]{:S(2)}) async-start(), calls=%async_computation | async-start | bytes 1572864 | tf_op jit(solution)/shard_map/psum | solution.py:173
  1628.0 235.7 %all-reduce.103.cloned.1.call-start = ((), (), s32[]{:S(2)}) async-start(), calls=%async_computation.5 | async-start | bytes 4194304 | tf_op jit(solution)/shard_map/psum | solution.py:197
  (154 other events, 5188.8 us)
Sparse Core Ops, SparseCore 0:
  111.1 78.1 all-reduce.100
  1116.8 81.4 all-reduce.98
  1284.5 84.6 all-reduce.96
  1457.0 84.5 all-reduce.94
  1628.1 84.3 all-reduce.92
  1751.4 112.2 all-reduce.102
where the time goes:
time: 1890 us; the launch traced here: 1880 us
  blocking collectives  936 us (50%)
  waiting for transfers between devices  366 us (19%)
  starting transfers between devices  191 us (10%)
  local copies, waits for them, and re-layouts  169 us (9%)
  matrix products  138 us (7%)
  other arithmetic  56.4 us (3%)
  between operations  19 us (1%)
    unnamed x24, blocking collectives  494 us
    psum x5, waiting for transfers between devices, per_device(): lax.psum((mm_last(grad_rows, wd), mm_last(grad_rows, bd)), 'tensor')  254 us
    all_gather x10, blocking collectives, gather_rows(): return lax.all_gather(value, 'dp', axis=0, tiled=True)  244 us
    unnamed x56, starting transfers between devices  172 us
    unnamed x294, local copies, waits for them, and re-layouts  137 us
    all_gather x5, blocking collectives, per_device(): masked_all = lax.all_gather(masked_q, 'tensor', axis=0, tiled=True)  104 us
    psum x1, waiting for transfers between devices, per_device(): grad_au, grad_bd = lax.psum((grad_au, grad_bd), 'dp')  103 us
    all_gather x5, blocking collectives, per_device(): forward_summed = lax.all_gather(summed_share, 'tensor', axis=0, tiled=True)  93.2 us
  transfers between devices with their start and end apart: 70, of which 9 were waited for; matrix products, arithmetic and copies ran while one was open for 25% of the time, Pallas kernels for 0%

commit v1 on v0

v1 whole, which is shorter than its diff:
```python
import jax
import jax.numpy as jnp
from jax import lax
from jax.sharding import PartitionSpec as P

D = 8192
RMAX = 64
JOBS = 4
MB = 2
SEQ_LEN = 12
CHIPS = 4
CORES = 2

EPS = 1e-05
ALPHA = 16.0

BF = jnp.bfloat16
F32 = jnp.float32
Z_GROUPS = [[0, 2, 4, 6], [1, 3, 5, 7]]


def column_weights(ranks, lanes):
    column = jnp.arange(lanes, dtype=jnp.int32)
    col_job = column // RMAX
    picked = col_job[:, None] == jnp.arange(JOBS, dtype=jnp.int32)[None, :]
    rank_col = jnp.sum(jnp.where(picked, ranks[None, :], 0), axis=1)
    scale = jnp.where(
        column % RMAX < rank_col, ALPHA / rank_col.astype(jnp.float32), jnp.float32(0.0)
    )
    return (col_job, scale)


def silu_grad(u):
    sig = jax.nn.sigmoid(u)
    return sig * (1.0 + u * (1.0 - sig))


def mm(left, right):
    return jnp.dot(left, right, preferred_element_type=F32)


def mm_last(left, right):
    return lax.dot_general(left, right, (((1,), (1,)), ((), ())), preferred_element_type=F32)


def mm_first(left, right):
    return lax.dot_general(left, right, (((0,), (0,)), ((), ())), preferred_element_type=F32)


def core_swap(value):
    devices = lax.axis_size("tensor")
    return lax.ppermute(value, "tensor", [(i, i ^ 1) for i in range(devices)])


def z_exchange(value):
    return lax.all_to_all(value, "tensor", 0, 0, axis_index_groups=Z_GROUPS)


def dp_exchange(value):
    return lax.all_to_all(value, "dp", 0, 0)


def pipe_shift(value, step):
    n = lax.axis_size("pipe")
    return lax.ppermute(value, "pipe", [(i, (i + step) % n) for i in range(n)])


def two_terms(value):
    high = lax.reduce_precision(value, 8, 7)
    low = value - high
    return jnp.pad(jnp.stack([high, low], axis=1), ((0, 0), (0, 126)))


def sum_over_tensor(product, rows):
    half = rows.shape[0] // CORES
    got = core_swap(product(rows[half:]).astype(BF))
    part = (product(rows[:half]) + got.astype(F32)).astype(BF)
    parts = z_exchange(part.reshape(CHIPS, half // CHIPS, part.shape[1]))
    return jnp.sum(parts.astype(F32), axis=0)


def gather_tensor(value):
    first = z_exchange(value)
    first = first.reshape(CHIPS * first.shape[1], first.shape[2])
    return first, core_swap(first)


def to_chips(value):
    return jnp.broadcast_to(value[None], (CHIPS,) + value.shape)


def sum_over_dp(product, first, second):
    parts = [product(first).astype(BF), product(second).astype(BF)]
    n = lax.axis_size("dp")
    rows = first.shape[0] * CORES // n
    parts = [p.reshape(n // CORES, rows, p.shape[1]) for p in parts]
    return jnp.sum(dp_exchange(jnp.concatenate(parts, axis=0)).astype(F32), axis=0)


def gather_dp(value):
    n = lax.axis_size("dp")
    got = dp_exchange(jnp.broadcast_to(value[None], (n,) + value.shape))
    return got.reshape(n * value.shape[0], value.shape[1])


def per_device(h_in, cotangent, w_up, w_down, a_up, b_up, a_down, b_down, job_ids, ranks):
    wu, wd, au, bu, ad, bd = (w_up[0], w_down[0], a_up[0], b_up[0], a_down[0], b_down[0])
    width = h_in.shape[2]
    hidden = wu.shape[1]
    lanes = au.shape[1]
    replicas = lax.axis_size("dp")
    sections = lax.axis_size("pipe")
    section = lax.axis_index("pipe")
    place = lax.axis_index("dp")
    chip = lax.axis_index("tensor") // CORES
    core = lax.axis_index("tensor") % CORES
    rows = MB * h_in.shape[1]
    turn = core * (replicas // CORES)
    col_job, scale = column_weights(ranks, lanes)

    def mask_of(position):
        jobs = lax.dynamic_slice_in_dim(job_ids, (position + turn) % replicas, 1, 1)
        jobs = jnp.broadcast_to(jobs, (MB, SEQ_LEN)).reshape(-1)
        return jnp.where(jobs[:, None] == col_job[None, :], scale[None, :], F32(0.0))

    mask_share = mask_of(chip)
    mask_own = mask_of(place)

    both = jnp.concatenate([h_in.reshape(rows, width), cotangent.reshape(rows, width)], axis=1)
    both = gather_dp(both)
    half = both.shape[0] // CORES
    both = jnp.where(core == 0, both, jnp.concatenate([both[half:], both[:half]], axis=0))
    x_first = both[:, :width]
    g_first = both[:, width:]
    x_first_own = lax.dynamic_slice_in_dim(x_first, place * rows, rows, 0)
    g_first_own = lax.dynamic_slice_in_dim(g_first, place * rows, rows, 0)

    def up(x):
        ss = jnp.sum(jnp.square(x.astype(F32)), axis=1)
        return jnp.concatenate([mm(x, wu), mm(x, au), two_terms(ss)], axis=1)

    def up_back(g):
        return jnp.concatenate([mm_last(g, wd), mm_last(g, bd)], axis=1)

    def activate(summed):
        rs = lax.rsqrt((summed[:, hidden + lanes] + summed[:, hidden + lanes + 1]) / D + EPS)
        qb = (summed[:, hidden : hidden + lanes] * mask_share).astype(BF)
        pre = summed[:, :hidden] + mm(qb, bu)
        u = rs[:, None] * pre
        return rs, qb, pre, u, jax.nn.silu(u).astype(BF)

    def down(act):
        return jnp.concatenate([mm(act, wd), mm(act, ad)], axis=1)

    x_own, x = x_first_own, x_first
    for tick in range(sections - 1):
        with jax.named_scope("forward"):
            act = activate(sum_over_tensor(up, x))[-1]
            first, second = gather_tensor(to_chips(act))
            y = sum_over_dp(down, first, second)
            rb = (y[:, width:] * mask_own).astype(BF)
            h_next = (x_own.astype(F32) + y[:, :width] + mm(rb, bd)).astype(BF)
            x_own = jnp.where(section == 0, x_first_own, pipe_shift(h_next, 1))
            x = gather_dp(x_own)

    with jax.named_scope("turn"):

        def up_both(pair):
            return jnp.concatenate([up(pair[:, :width]), up_back(pair[:, width:])], axis=1)

        summed = sum_over_tensor(up_both, jnp.concatenate([x, g_first], axis=1))
        split = hidden + lanes + 128
        rs, qb, pre, u, act = activate(summed[:, :split])
        slope = silu_grad(u)
        d_sum = summed[:, split:]

    def hidden_grads(d_sum):
        d_rb = (d_sum[:, hidden:] * mask_share).astype(BF)
        d_u = (d_sum[:, :hidden] + mm_last(d_rb, ad)) * slope
        return d_rb, d_u, (d_u * rs[:, None]).astype(BF)

    g_own, g = g_first_own, g_first
    for tick in range(sections - 1):
        with jax.named_scope("backward"):
            d_rb, d_u, d_sb = hidden_grads(d_sum)
            factor = (rs**3 / D) * jnp.sum(d_u * pre, axis=1)
            sent = jnp.concatenate([d_sb, two_terms(factor).astype(BF)], axis=1)
            first, second = gather_tensor(to_chips(sent))

            def back(both):
                block, inputs = both[:, : hidden + 128], both[:, hidden + 128 :]
                d_s = block[:, :hidden]
                factors = block[:, hidden : hidden + 2].astype(F32)
                factors = (factors[:, 0] + factors[:, 1])[:, None]
                d_x = mm_last(d_s, wu) - inputs.astype(F32) * factors
                return jnp.concatenate([d_x, mm_last(d_s, bu)], axis=1)

            half = x.shape[0] // CORES
            d = sum_over_dp(
                back,
                jnp.concatenate([first, x[:half]], axis=1),
                jnp.concatenate([second, x[half:]], axis=1),
            )
            d_qb = (d[:, width:] * mask_own).astype(BF)
            d_x = (g_own.astype(F32) + d[:, :width] + mm_last(d_qb, au)).astype(BF)
            g_own = jnp.where(section == sections - 1, g_first_own, pipe_shift(d_x, -1))
            g = gather_dp(g_own)
            d_sum = sum_over_tensor(up_back, g)

    with jax.named_scope("last"):
        d_rb, d_u, d_sb = hidden_grads(d_sum)

        def by_chip(value):
            return jnp.swapaxes(value.reshape(value.shape[0], CHIPS, lanes // CHIPS), 0, 1)

        sent = [to_chips(d_sb), to_chips(act), by_chip(qb), by_chip(d_rb)]
        first, second = gather_tensor(jnp.concatenate(sent, axis=2))

        def adapters(block):
            d_s, a = block[:, :hidden], block[:, hidden : 2 * hidden]
            return jnp.concatenate([mm_last(d_s, bu), mm(a, ad)], axis=1)

        sums = sum_over_dp(adapters, first, second)
        sums = (sums * jnp.concatenate([mask_own, mask_own], axis=1)).astype(BF)
        gathered = gather_dp(sums)
        d_qb, rb = gathered[:, :lanes], gathered[:, lanes:]
        grad_au = mm_first(x, d_qb)
        grad_bd = mm_first(rb, g)
        whole = jnp.concatenate([first, second], axis=0)
        d_sb, act = whole[:, :hidden], whole[:, hidden : 2 * hidden]
        group = lanes // CHIPS
        piece = group // CORES
        qb = whole[:, 2 * hidden : 2 * hidden + group]
        d_rb = whole[:, 2 * hidden + group :]
        grad_bu = lax.dynamic_slice_in_dim(mm_first(qb, d_sb), core * piece, piece, 0)
        grad_ad = mm_first(act, d_rb)
        grad_ad = jnp.where(core == 0, grad_ad[:, :piece], grad_ad[:, piece:])
    return (grad_au[None], grad_bu[None], grad_ad[None], grad_bd[None])


def solution(mesh):
    in_specs = (
        P(None, "dp", "tensor"),
        P(None, "dp", "tensor"),
        P("pipe", "tensor", "dp"),
        P("pipe", "dp", "tensor"),
        P("pipe", "tensor", None),
        P("pipe", None, "dp"),
        P("pipe", "dp", None),
        P("pipe", None, "tensor"),
        P(),
        P(),
    )
    out_specs = (
        P("pipe", "tensor", None),
        P("pipe", "tensor", "dp"),
        P("pipe", "dp", "tensor"),
        P("pipe", None, "tensor"),
    )
    return jax.shard_map(
        per_device, mesh=mesh, in_specs=in_specs, out_specs=out_specs, check_vma=False
    )
```

time: 1890 us -> 597 us (0.32)
  blocking collectives: 936 us -> 292 us
  waiting for transfers between devices: 366 us -> 88.7 us
  local copies, waits for them, and re-layouts: 169 us -> 14.7 us
  starting transfers between devices: 191 us -> 76.4 us
  matrix products: 138 us -> 84.6 us
  other arithmetic: 56.4 us -> 27 us
    unnamed x24 -> x0, blocking collectives: 494 us -> none
    all_gather x20 -> x0, blocking collectives: 442 us -> none  [the longest x10 244 us: gather_rows(): return lax.all_gather(value, 'dp', axis=0, tiled=True)]
    psum x6 -> x0, waiting for transfers between devices: 357 us -> none  [the longest x5 254 us: per_device(): lax.psum((mm_last(grad_rows, wd), mm_last(grad_rows, bd)), 'tensor')]
    all_to_all x0 -> x22, blocking collectives: none -> 292 us  [the longest x11 171 us: z_exchange(): return lax.all_to_all(value, 'tensor', 0, 0, axis_index_groups=Z_GROUPS)]
    unnamed x56 -> x0, starting transfers between devices: 172 us -> none
    unnamed x294 -> x83, local copies, waits for them, and re-layouts: 137 us -> 4.68 us
    all_to_all x0 -> x7, waiting for transfers between devices: none -> 70.1 us  [the longest x3 41.8 us: z_exchange(): return lax.all_to_all(value, 'tensor', 0, 0, axis_index_groups=Z_GROUPS)]
    all_to_all x0 -> x7, starting transfers between devices: none -> 32.7 us  [the longest x4 17.7 us: dp_exchange(): return lax.all_to_all(value, 'dp', 0, 0)]
  transfers between devices with their start and end apart: 70 -> 27, of which waited for: 9 -> 17; matrix products, arithmetic and copies ran while one was open for 25% -> 7% of each run, Pallas kernels for 0% -> 0%
where the time goes in v1:
time: 597 us; the launch traced here: 586 us
  blocking collectives  292 us (49%)
  waiting for transfers between devices  88.7 us (15%)
  matrix products  84.6 us (14%)
  starting transfers between devices  76.4 us (13%)
  other arithmetic  27 us (5%)
  local copies, waits for them, and re-layouts  14.7 us (2%)
    all_to_all x11, blocking collectives, z_exchange(): return lax.all_to_all(value, 'tensor', 0, 0, axis_index_groups=Z_GROUPS)  171 us
    all_to_all x11, blocking collectives, dp_exchange(): return lax.all_to_all(value, 'dp', 0, 0)  121 us
    dot_general x37, matrix products, mm_last(): lax.dot_general(left, right, (((1,), (1,)), ((), ())), preferred_element_...  47.9 us
    all_to_all x3, waiting for transfers between devices, z_exchange(): return lax.all_to_all(value, 'tensor', 0, 0, axis_index_groups=Z_GROUPS)  41.8 us
    ppermute x14, starting transfers between devices, core_swap(): return lax.ppermute(value, 'tensor', [(i, i ^ 1) for i in range(devices)])  38.4 us
    dot_general x37, matrix products, mm(): return jnp.dot(left, right, preferred_element_type=F32)  33.5 us
    all_to_all x4, waiting for transfers between devices, dp_exchange(): return lax.all_to_all(value, 'dp', 0, 0)  28.3 us
    all_to_all x4, starting transfers between devices, dp_exchange(): return lax.all_to_all(value, 'dp', 0, 0)  17.7 us
  transfers between devices with their start and end apart: 27, of which 17 were waited for; matrix products, arithmetic and copies ran while one was open for 7% of the time, Pallas kernels for 0%

profile of v1, /device:TPU:1, one launch (start us, length us, event | category | flops | bytes accessed | tf_op | source)
XLA Modules:
  0.0 585.8 jit_solution(2686957140564652273)
XLA Ops:
  9.7 11.7 %all-to-all-done = bf16[8,24,2048]{2,1,0:T(8,128)(2,1)S(1)} async-done(((bf16[8,24,2048]{2,1,0:T(8,128)(2,1)}), bf16[8,24,2048]{2,1,0:T(8,128)(2,1)S(1)}, u32[]{:S(2)}, u32[]{:S(2)}) %all-to-all-start) | async-done | bytes 786464 | tf_op jit(solution)/shard_map/all_to_all | solution.py:60
  40.8 12.2 %all-to-all-done.1 = bf16[4,24,2176]{2,1,0:T(8,128)(2,1)} async-done(((bf16[4,24,2176]{2,1,0:T(8,128)(2,1)}), bf16[4,24,2176]{2,1,0:T(8,128)(2,1)}, u32[]{:S(2)}, u32[]{:S(2)}) %all-to-all-start.1) | async-done | bytes 417824 | tf_op jit(solution)/shard_map/forward/all_to_all | solution.py:56
  54.7 14.7 %all_to_all.145 = bf16[4,24,1792]{2,1,0:T(8,128)(2,1)S(1)} all-to-all(bf16[4,24,1792]{2,1,0:T(8,128)(2,1)S(1)} %broadcast_in_dim.88), channel_id=1, replica_groups={{0,2,4,6},{1,3,5,7},{8,10,12,14},{9,11,13,15},{16,18,20,22},{17,19,21,2..., dimensions={0} | all-to-all | bytes 688128 | tf_op jit(solution)/shard_map/forward/all_to_all | solution.py:56
  94.2 10.2 %all_to_all.146 = bf16[8,24,1024]{2,1,0:T(8,128)(2,1)S(1)} all-to-all(bf16[8,24,1024]{2,1,0:T(8,128)(2,1)S(1)} %broadcast_in_dim.91), channel_id=1, replica_groups=mesh['dp'=8,'pipe'=4,'tensor'=8] {'dp'}, dimensions={0} | all-to-all | bytes 786432 | tf_op jit(solution)/shard_map/forward/all_to_all | solution.py:60
  118.9 15.9 %all_to_all.147 = bf16[4,24,2176]{2,1,0:T(8,128)(2,1)S(1)} all-to-all(bf16[4,24,2176]{2,1,0:T(8,128)(2,1)S(1)} %bitcast.441), channel_id=1, replica_groups={{0,2,4,6},{1,3,5,7},{8,10,12,14},{9,11,13,15},{16,18,20,22},{17,19,21,2..., dimensions={0} | all-to-all | bytes 835584 | tf_op jit(solution)/shard_map/forward/all_to_all | solution.py:56
  135.4 13.2 %all_to_all.148 = bf16[4,24,1792]{2,1,0:T(8,128)(2,1)S(1)} all-to-all(bf16[4,24,1792]{2,1,0:T(8,128)(2,1)S(1)} %broadcast_in_dim.92), channel_id=1, replica_groups={{0,2,4,6},{1,3,5,7},{8,10,12,14},{9,11,13,15},{16,18,20,22},{17,19,21,2..., dimensions={0} | all-to-all | bytes 688128 | tf_op jit(solution)/shard_map/forward/all_to_all | solution.py:56
  153.7 12.4 %all_to_all.149 = bf16[8,24,1280]{2,1,0:T(8,128)(2,1)S(1)} all-to-all(bf16[8,24,1280]{2,1,0:T(8,128)(2,1)S(1)} %maximum_maximum_fusion.1), channel_id=1, replica_groups=mesh['dp'=8,'pipe'=4,'tensor'=8] {'dp'}, dimensions={0} | all-to-all | bytes 983040 | tf_op jit(solution)/shard_map/forward/all_to_all | solution.py:60
  171.5 9.8 %all_to_all.150 = bf16[8,24,1024]{2,1,0:T(8,128)(2,1)S(1)} all-to-all(bf16[8,24,1024]{2,1,0:T(8,128)(2,1)S(1)} %broadcast_in_dim.93), channel_id=1, replica_groups=mesh['dp'=8,'pipe'=4,'tensor'=8] {'dp'}, dimensions={0} | all-to-all | bytes 786432 | tf_op jit(solution)/shard_map/forward/all_to_all | solution.py:60
  194.5 16.1 %all_to_all.151 = bf16[4,24,2176]{2,1,0:T(8,128)(2,1)S(1)} all-to-all(bf16[4,24,2176]{2,1,0:T(8,128)(2,1)S(1)} %bitcast.442), channel_id=1, replica_groups={{0,2,4,6},{1,3,5,7},{8,10,12,14},{9,11,13,15},{16,18,20,22},{17,19,21,2..., dimensions={0} | all-to-all | bytes 835584 | tf_op jit(solution)/shard_map/forward/all_to_all | solution.py:56
  211.2 13.8 %all_to_all.152 = bf16[4,24,1792]{2,1,0:T(8,128)(2,1)S(1)} all-to-all(bf16[4,24,1792]{2,1,0:T(8,128)(2,1)S(1)} %broadcast_in_dim.94), channel_id=1, replica_groups={{0,2,4,6},{1,3,5,7},{8,10,12,14},{9,11,13,15},{16,18,20,22},{17,19,21,2..., dimensions={0} | all-to-all | bytes 688128 | tf_op jit(solution)/shard_map/forward/all_to_all | solution.py:56
  229.7 12.3 %all_to_all.153 = bf16[8,24,1280]{2,1,0:T(8,128)(2,1)S(1)} all-to-all(bf16[8,24,1280]{2,1,0:T(8,128)(2,1)S(1)} %maximum_maximum_fusion.2), channel_id=1, replica_groups=mesh['dp'=8,'pipe'=4,'tensor'=8] {'dp'}, dimensions={0} | all-to-all | bytes 983040 | tf_op jit(solution)/shard_map/forward/all_to_all | solution.py:60
  247.4 9.8 %all_to_all.154 = bf16[8,24,1024]{2,1,0:T(8,128)(2,1)S(1)} all-to-all(bf16[8,24,1024]{2,1,0:T(8,128)(2,1)S(1)} %broadcast_in_dim.95), channel_id=1, replica_groups=mesh['dp'=8,'pipe'=4,'tensor'=8] {'dp'}, dimensions={0} | all-to-all | bytes 786432 | tf_op jit(solution)/shard_map/forward/all_to_all | solution.py:60
  284.0 24.3 %all_to_all.155 = bf16[4,24,4224]{2,1,0:T(8,128)(2,1)S(1)} all-to-all(bf16[4,24,4224]{2,1,0:T(8,128)(2,1)S(1)} %bitcast.401), channel_id=1, replica_groups={{0,2,4,6},{1,3,5,7},{8,10,12,14},{9,11,13,15},{16,18,20,22},{17,19,21,2..., dimensions={0} | all-to-all | bytes 1622016 | tf_op jit(solution)/shard_map/turn/all_to_all | solution.py:56
  312.7 13.6 %all_to_all.156 = bf16[4,24,1920]{2,1,0:T(8,128)(2,1)S(1)} all-to-all(bf16[4,24,1920]{2,1,0:T(8,128)(2,1)S(1)} %broadcast_in_dim.96), channel_id=1, replica_groups={{0,2,4,6},{1,3,5,7},{8,10,12,14},{9,11,13,15},{16,18,20,22},{17,19,21,2..., dimensions={0} | all-to-all | bytes 737280 | tf_op jit(solution)/shard_map/backward/all_to_all | solution.py:56
  336.1 12.1 %all_to_all.157 = bf16[8,24,1280]{2,1,0:T(8,128)(2,1)S(1)} all-to-all(bf16[8,24,1280]{2,1,0:T(8,128)(2,1)S(1)} %maximum_maximum_fusion.3), channel_id=1, replica_groups=mesh['dp'=8,'pipe'=4,'tensor'=8] {'dp'}, dimensions={0} | all-to-all | bytes 983040 | tf_op jit(solution)/shard_map/backward/all_to_all | solution.py:60
  371.7 15.3 %all_to_all.159 = bf16[4,24,2048]{2,1,0:T(8,128)(2,1)S(1)} all-to-all(bf16[4,24,2048]{2,1,0:T(8,128)(2,1)S(1)} %bitcast.445), channel_id=1, replica_groups={{0,2,4,6},{1,3,5,7},{8,10,12,14},{9,11,13,15},{16,18,20,22},{17,19,21,2..., dimensions={0} | all-to-all | bytes 786432 | tf_op jit(solution)/shard_map/backward/all_to_all | solution.py:56
  389.2 15.2 %all_to_all.160 = bf16[4,24,1920]{2,1,0:T(8,128)(2,1)S(1)} all-to-all(bf16[4,24,1920]{2,1,0:T(8,128)(2,1)S(1)} %broadcast_in_dim.98), channel_id=1, replica_groups={{0,2,4,6},{1,3,5,7},{8,10,12,14},{9,11,13,15},{16,18,20,22},{17,19,21,2..., dimensions={0} | all-to-all | bytes 737280 | tf_op jit(solution)/shard_map/backward/all_to_all | solution.py:56
  412.6 12.4 %all_to_all.161 = bf16[8,24,1280]{2,1,0:T(8,128)(2,1)S(1)} all-to-all(bf16[8,24,1280]{2,1,0:T(8,128)(2,1)S(1)} %maximum_maximum_fusion.4), channel_id=1, replica_groups=mesh['dp'=8,'pipe'=4,'tensor'=8] {'dp'}, dimensions={0} | all-to-all | bytes 983040 | tf_op jit(solution)/shard_map/backward/all_to_all | solution.py:60
  429.3 9.8 %all_to_all.162 = bf16[8,24,1024]{2,1,0:T(8,128)(2,1)S(1)} all-to-all(bf16[8,24,1024]{2,1,0:T(8,128)(2,1)S(1)} %broadcast_in_dim.99), channel_id=1, replica_groups=mesh['dp'=8,'pipe'=4,'tensor'=8] {'dp'}, dimensions={0} | all-to-all | bytes 786432 | tf_op jit(solution)/shard_map/backward/all_to_all | solution.py:60
  445.4 15.1 %all_to_all.163 = bf16[4,24,2048]{2,1,0:T(8,128)(2,1)S(1)} all-to-all(bf16[4,24,2048]{2,1,0:T(8,128)(2,1)S(1)} %bitcast.446), channel_id=1, replica_groups={{0,2,4,6},{1,3,5,7},{8,10,12,14},{9,11,13,15},{16,18,20,22},{17,19,21,2..., dimensions={0} | all-to-all | bytes 786432 | tf_op jit(solution)/shard_map/backward/all_to_all | solution.py:56
  462.8 14.4 %all_to_all.164 = bf16[4,24,1920]{2,1,0:T(8,128)(2,1)S(1)} all-to-all(bf16[4,24,1920]{2,1,0:T(8,128)(2,1)S(1)} %broadcast_in_dim.100), channel_id=1, replica_groups={{0,2,4,6},{1,3,5,7},{8,10,12,14},{9,11,13,15},{16,18,20,22},{17,19,21,2..., dimensions={0} | all-to-all | bytes 737280 | tf_op jit(solution)/shard_map/backward/all_to_all | solution.py:56
  485.9 12.4 %all_to_all.165 = bf16[8,24,1280]{2,1,0:T(8,128)(2,1)S(1)} all-to-all(bf16[8,24,1280]{2,1,0:T(8,128)(2,1)S(1)} %maximum_maximum_fusion.5), channel_id=1, replica_groups=mesh['dp'=8,'pipe'=4,'tensor'=8] {'dp'}, dimensions={0} | all-to-all | bytes 983040 | tf_op jit(solution)/shard_map/backward/all_to_all | solution.py:60
  522.9 12.1 %all-to-all-done.25 = bf16[4,24,2048]{2,1,0:T(8,128)(2,1)S(1)} async-done(((bf16[4,24,2048]{2,1,0:T(8,128)(2,1)}), bf16[4,24,2048]{2,1,0:T(8,128)(2,1)S(1)}, u32[]{:S(2)}, u32[]{:S(2)}) %all-to-all-start.25) | async-done | bytes 393248 | tf_op jit(solution)/shard_map/backward/all_to_all | solution.py:56
  540.9 17.5 %all-to-all-done.26 = bf16[4,24,3712]{2,1,0:T(8,128)(2,1)S(1)} async-done(((bf16[4,24,3712]{2,1,0:T(8,128)(2,1)}), bf16[4,24,3712]{2,1,0:T(8,128)(2,1)S(1)}, u32[]{:S(2)}, u32[]{:S(2)}) %all-to-all-start.26) | async-done | bytes 712736 | tf_op jit(solution)/shard_map/last/all_to_all | solution.py:56
  (369 shorter events, 257.4 us)
Async XLA Ops:
  3.5 17.9 %all-to-all-start = ((bf16[8,24,2048]{2,1,0:T(8,128)(2,1)}), bf16[8,24,2048]{2,1,0:T(8,128)(2,1)S(1)}, u32[]{:S(2)}, u32[]{:S(2)}) async-start(bf16[8,24,2048]{2,1,0:T(8,128)(2,1)} %broadcast_in_dim.80), calls=%async_computation | async-start | bytes 1572864 | tf_op jit(solution)/shard_map/all_to_all | solution.py:60
  26.1 5.1 collective-permute-start
  33.0 20.0 %all-to-all-start.1 = ((bf16[4,24,2176]{2,1,0:T(8,128)(2,1)}), bf16[4,24,2176]{2,1,0:T(8,128)(2,1)}, u32[]{:S(2)}, u32[]{:S(2)}) async-start(bf16[4,24,2176]{2,1,0:T(8,128)(2,1)} %bitcast.440), calls=%async_computation.1 | async-start | bytes 835584 | tf_op jit(solution)/shard_map/forward/all_to_all | solution.py:56
  69.4 4.2 collective-permute-start.1
  75.4 12.6 %all-to-all-start.3 = ((bf16[8,24,1280]{2,1,0:T(8,128)(2,1)}), bf16[8,24,1280]{2,1,0:T(8,128)(2,1)S(1)}, u32[]{:S(2)}, u32[]{:S(2)}) async-start(bf16[8,24,1280]{2,1,0:T(8,128)(2,1)} %maximum_maximum_fusion), calls=%async_computation.3 | async-start | bytes 983040 | tf_op jit(solution)/shard_map/forward/all_to_all | solution.py:60
  89.1 4.3 collective-permute-start.2
  111.3 6.5 %collective-permute-start.3 = (bf16[96,2176]{1,0:T(8,128)(2,1)}, bf16[96,2176]{1,0:T(8,128)(2,1)}, u32[]{:S(2)}, u32[]{:S(2)}) collective-permute-start(bf16[96,2176]{1,0:T(8,128)(2,1)} %fusion.234), channel_id=1, source_target_pairs={{0,1},{1,0},{2,3},{3,2},{4,5},{5,4},{6,7},{7,6},{8,9},{9,8},{10,11... | collective-permute-start | bytes 1253384 | tf_op jit(solution)/shard_map/forward/ppermute | solution.py:52
  148.6 4.0 collective-permute-start.4
  166.5 4.2 collective-permute-start.5
  186.1 7.2 %collective-permute-start.6 = (bf16[96,2176]{1,0:T(8,128)(2,1)}, bf16[96,2176]{1,0:T(8,128)(2,1)}, u32[]{:S(2)}, u32[]{:S(2)}) collective-permute-start(bf16[96,2176]{1,0:T(8,128)(2,1)} %fusion.235), channel_id=1, source_target_pairs={{0,1},{1,0},{2,3},{3,2},{4,5},{5,4},{6,7},{7,6},{8,9},{9,8},{10,11... | collective-permute-start | bytes 1253384 | tf_op jit(solution)/shard_map/forward/ppermute | solution.py:52
  225.0 3.6 collective-permute-start.7
  242.4 4.2 collective-permute-start.8
  271.2 11.0 %collective-permute-start.9 = (bf16[96,4224]{1,0:T(8,128)(2,1)}, bf16[96,4224]{1,0:T(8,128)(2,1)}, u32[]{:S(2)}, u32[]{:S(2)}) collective-permute-start(bf16[96,4224]{1,0:T(8,128)(2,1)} %fusion.155), channel_id=1, source_target_pairs={{0,1},{1,0},{2,3},{3,2},{4,5},{5,4},{6,7},{7,6},{8,9},{9,8},{10,11... | collective-permute-start | bytes 2433032 | tf_op jit(solution)/shard_map/turn/ppermute | solution.py:52
  326.3 7.8 %collective-permute-start.10 = (bf16[96,1920]{1,0:T(8,128)(2,1)S(1)}, bf16[96,1920]{1,0:T(8,128)(2,1)S(1)}, u32[]{:S(2)}, u32[]{:S(2)}) collective-permute-start(bf16[96,1920]{1,0:T(8,128)(2,1)S(1)} %bitcast.406), channel_id=1, source_target_pairs={{0,1},{1,0},{2,3},{3,2},{4,5},{5,4},{6,7},{7,6},{8,9},{9,8},{10,11... | collective-permute-start | bytes 1105928 | tf_op jit(solution)/shard_map/backward/ppermute | solution.py:52
  366.9 4.6 collective-permute-start.12
  404.3 6.2 %collective-permute-start.13 = (bf16[96,1920]{1,0:T(8,128)(2,1)S(1)}, bf16[96,1920]{1,0:T(8,128)(2,1)S(1)}, u32[]{:S(2)}, u32[]{:S(2)}) collective-permute-start(bf16[96,1920]{1,0:T(8,128)(2,1)S(1)} %bitcast.410), channel_id=1, source_target_pairs={{0,1},{1,0},{2,3},{3,2},{4,5},{5,4},{6,7},{7,6},{8,9},{9,8},{10,11... | collective-permute-start | bytes 1105928 | tf_op jit(solution)/shard_map/backward/ppermute | solution.py:52
  440.7 4.6 collective-permute-start.15
  477.2 6.7 %collective-permute-start.16 = (bf16[96,1920]{1,0:T(8,128)(2,1)S(1)}, bf16[96,1920]{1,0:T(8,128)(2,1)S(1)}, u32[]{:S(2)}, u32[]{:S(2)}) collective-permute-start(bf16[96,1920]{1,0:T(8,128)(2,1)S(1)} %bitcast.402), channel_id=1, source_target_pairs={{0,1},{1,0},{2,3},{3,2},{4,5},{5,4},{6,7},{7,6},{8,9},{9,8},{10,11... | collective-permute-start | bytes 1105928 | tf_op jit(solution)/shard_map/backward/ppermute | solution.py:52
  498.6 3.3 collective-permute-start.17
  514.1 4.4 collective-permute-start.18
  519.3 15.7 %all-to-all-start.25 = ((bf16[4,24,2048]{2,1,0:T(8,128)(2,1)}), bf16[4,24,2048]{2,1,0:T(8,128)(2,1)S(1)}, u32[]{:S(2)}, u32[]{:S(2)}) async-start(bf16[4,24,2048]{2,1,0:T(8,128)(2,1)} %bitcast.61), calls=%async_computation.25 | async-start | bytes 786432 | tf_op jit(solution)/shard_map/backward/all_to_all | solution.py:56
  536.7 21.7 %all-to-all-start.26 = ((bf16[4,24,3712]{2,1,0:T(8,128)(2,1)}), bf16[4,24,3712]{2,1,0:T(8,128)(2,1)S(1)}, u32[]{:S(2)}, u32[]{:S(2)}) async-start(bf16[4,24,3712]{2,1,0:T(8,128)(2,1)} %concatenate.224), calls=%async_computation.26 | async-start | bytes 1425408 | tf_op jit(solution)/shard_map/last/all_to_all | solution.py:56
  562.3 10.7 %all-to-all-start.27 = ((bf16[8,24,512]{2,1,0:T(8,128)(2,1)}), bf16[8,24,512]{2,1,0:T(8,128)(2,1)S(1)}, u32[]{:S(2)}, u32[]{:S(2)}) async-start(bf16[8,24,512]{2,1,0:T(8,128)(2,1)} %maximum_maximum_fusion.6), calls=%async_computation.27 | async-start | bytes 393216 | tf_op jit(solution)/shard_map/last/all_to_all | solution.py:60
  573.8 9.1 %all-to-all-start.28 = ((bf16[8,24,512]{2,1,0:T(8,128)(2,1)}), bf16[8,24,512]{2,1,0:T(8,128)(2,1)S(1)}, u32[]{:S(2)}, u32[]{:S(2)}) async-start(bf16[8,24,512]{2,1,0:T(8,128)(2,1)} %broadcast_in_dim.104), calls=%async_computation.28 | async-start | bytes 393216 | tf_op jit(solution)/shard_map/last/all_to_all | solution.py:60
  (37 other events, 645.1 us)
